TPU v7x, 32 devices: a whole 2x2x4 slice. The times are simulated.
32 devices in a mesh: grp: 2 (over x), row: 16 (over z, y, core).
Axes of the slice: x: 2, y: 2, z: 4, core: 2. Of those that a mesh axis runs over, the one named last changes fastest.
Arguments:
- prints_a: int32 [5120, 4], P(('grp', 'row')), parts along dimension 0, may hold values from 0 to 1073741823, as said below
- prints_b: int32 [5120, 4], P(('grp', 'row')), parts along dimension 0, may hold values from 0 to 1073741823, as said below
- prints_c: int32 [5120, 4], P(('grp', 'row')), parts along dimension 0, may hold values from 0 to 1073741823, as said below
- prints_d: int32 [5120, 4], P(('grp', 'row')), parts along dimension 0, may hold values from 0 to 1073741823, as said below
- start_block: float32 [5120, 64], P(('grp', 'row')), parts along dimension 0, may hold values from -6 to 6
Outputs:
- basis: float32 [5120, 64], P(('grp', 'row')), parts along dimension 0
There are 2 independent parts, one for each index of `grp`. A program takes and returns all parts, laid end to end along the dimension named above; each array names one. Nothing has to cross between parts.
Inputs may be any that keep to these rules, and one draw needn't show every extreme that they name: `prints_a`: every word lies below 2 to the 30th and word 0 of every molecule is nonzero, so every fingerprint has a set bit. `prints_b`: every word lies below 2 to the 30th. `prints_c`: every word lies below 2 to the 30th. `prints_d`: every word lies below 2 to the 30th.
All inputs are finite; a program needn't handle non-finite values.
Results may differ from a plain program's by a relative error of at most 0.0003.
Values sent between devices are 32-bit elements; how exact they have to be, the bound alone decides.
A program may use at most 128 MiB of HBM per device.

v0:
```python
import functools
import math

import jax
import jax.numpy as jnp
from jax import lax
from jax.experimental import pallas as pl
from jax.experimental.pallas import tpu as pltpu
from jax.sharding import PartitionSpec as P

F32 = jnp.float32
BF16 = jnp.bfloat16
HIGHEST = lax.Precision.HIGHEST
MESH = pl.DeviceIdType.MESH


def dot(left, right, dims, precision=None):
    return lax.dot_general(
        left, right, ((dims[:1], dims[1:]), ((), ())),
        precision=precision, preferred_element_type=F32,
    )


def swap(value):
    return pltpu.roll(value, 64, 1)


def low_lanes(shape):
    return lax.broadcasted_iota(jnp.int32, shape, 1) < 64


def split3(value):
    one = value.astype(BF16)
    rest = value - one.astype(F32)
    two = rest.astype(BF16)
    three = (rest - two.astype(F32)).astype(BF16)
    return one, two, three


def pack_rows(value):
    half = value.shape[0] // 2
    return jnp.where(low_lanes((half, 128)), value[:half], value[half:])


def bits_of(words):
    shift = lax.broadcasted_iota(jnp.int32, (words.shape[0], 32, words.shape[1]), 1)
    wide = jnp.broadcast_to(words[:, None, :], shift.shape)
    bits = jnp.bitwise_and(jnp.right_shift(wide, shift), 1).astype(F32)
    return bits.reshape(words.shape[0] * 32, words.shape[1])


def local_gram(packed):
    full = dot(packed, packed, (0, 0), HIGHEST)
    gram = full[:64] + swap(full[64:])
    return jnp.where(low_lanes((32, 128)), gram[:32], swap(gram[32:]))


def inverse_factor(gram):
    size = 64
    rows = lax.broadcasted_iota(jnp.int32, (size, 128), 0)
    lanes = lax.broadcasted_iota(jnp.int32, (size, 128), 1)
    low = lanes < size
    square = jnp.concatenate([gram, swap(gram)], axis=0)
    work = jnp.where(low, square, (lanes - size == rows).astype(F32))
    done = []
    for j in range(size):
        start = (j // 8) * 8
        top = j - start
        row = work[top : top + 1, :]
        column = jnp.broadcast_to(work[:, j : j + 1], work.shape)
        pivot = 1.0 / column[top : top + 1, :]
        index = lax.broadcasted_iota(jnp.int32, work.shape, 0) + start
        work = work - jnp.where(index > j, column, 0.0) * (pivot * row)
        if top == 7:
            done.append(work[:8])
            work = work[8:]
    work = jnp.concatenate(done, axis=0)
    diag = jnp.sum(jnp.where(lanes == rows, work, 0.0), axis=1, keepdims=True)
    inverse = work * (1.0 / jnp.sqrt(diag))
    return jnp.concatenate(
        [jnp.where(low, swap(inverse), 0.0), jnp.where(low, 0.0, inverse)], axis=0
    )


def kernel(
    lines, inner, rows, words_ref, start_ref, out_ref,
    words_i, words_j, block0, block1, kern, terms, stacked,
    row_parts, col_parts, send1, send2, part1, part2, gram1, gram2, gram3,
    send_sem, recv_sem,
):
    me = lax.axis_index("row")
    mine_a = me // inner
    mine_b = me % inner
    width = lines * rows
    half = rows // 2

    def inner_peer(step):
        slot = lax.rem(mine_b + step, inner)
        return slot, mine_a * inner + slot

    def line_peer(step):
        slot = lax.rem(mine_a + step, lines)
        return slot, slot * inner + mine_b

    barrier = pltpu.get_barrier_semaphore()
    for step in range(1, inner):
        pl.semaphore_signal(barrier, 1, device_id={"row": inner_peer(step)[1]}, device_id_type=MESH)
    for step in range(1, lines):
        pl.semaphore_signal(barrier, 1, device_id={"row": line_peer(step)[1]}, device_id_type=MESH)

    count = [0]
    started = []

    def exchange(size, peer, mine, buffer):
        waits = []
        for step in range(1, size):
            index = count[0]
            count[0] += 1
            target = peer(step)[1]
            copy = pltpu.make_async_remote_copy(
                src_ref=buffer.at[mine], dst_ref=buffer.at[mine],
                send_sem=send_sem.at[index], recv_sem=recv_sem.at[index],
                device_id={"row": target}, device_id_type=MESH,
            )
            copy.start()
            started.append(copy)
            slot = peer(size - step)[0]
            waits.append(
                pltpu.make_async_remote_copy(
                    src_ref=buffer.at[slot], dst_ref=buffer.at[slot],
                    send_sem=send_sem.at[index], recv_sem=recv_sem.at[index],
                    device_id={"row": target}, device_id_type=MESH,
                )
            )
        return waits

    def finish(waits):
        for copy in waits:
            copy.wait_recv()

    words_i[mine_b] = words_ref[...]
    words_j[mine_a] = words_ref[...]
    start = start_ref[...]
    block0[mine_a] = jnp.concatenate([start[:half], start[half:]], axis=1)

    pl.semaphore_wait(barrier, inner + lines - 2)
    wait_j = exchange(lines, line_peer, mine_a, words_j)
    wait_i = exchange(inner, inner_peer, mine_b, words_i)
    wait_x = exchange(lines, line_peer, mine_a, block0)

    finish(wait_j)
    right = bits_of(jnp.concatenate([words_j[d] for d in range(lines)], axis=1))
    count_j = jnp.sum(right, axis=0, keepdims=True)
    right = jnp.concatenate(
        [right.astype(BF16), jnp.ones((right.shape[0], 128), BF16)], axis=1
    )
    finish(wait_i)
    col_sum = jnp.zeros((8, width), F32)
    row_list = []
    for q in range(inner):
        left = bits_of(words_i[q]).astype(BF16)
        shared = dot(left, right, (0, 0))
        count_i = jnp.concatenate([shared[:, width:]] * (width // 128), axis=1)
        shared = shared[:, :width]
        tile = shared / (count_i + count_j - shared)
        kern[q * rows : (q + 1) * rows, :] = tile
        col_sum = col_sum + jnp.sum(tile.reshape(rows // 8, 8, width), axis=0)
        lane_sum = tile[:, :128]
        for piece in range(1, width // 128):
            lane_sum = lane_sum + tile[:, piece * 128 : (piece + 1) * 128]
        row_list.append(jnp.sum(lane_sum.T, axis=0, keepdims=True))
    row_parts[mine_b] = jnp.concatenate(row_list, axis=0)
    col_parts[mine_a] = jnp.sum(col_sum, axis=0, keepdims=True)
    wait_r = exchange(inner, inner_peer, mine_b, row_parts)
    wait_c = exchange(lines, line_peer, mine_a, col_parts)

    low = low_lanes((half, 128))

    def fill(block):
        for d in range(lines):
            one, two, three = [t.astype(F32) for t in split3(block[d])]
            base = d * rows
            stacked[base : base + half, :] = jnp.concatenate(
                [jnp.where(low, one, swap(two)), jnp.where(low, three, 0.0)], axis=1
            ).astype(BF16)
            stacked[base + half : base + rows, :] = jnp.concatenate(
                [jnp.where(low, swap(one), two), jnp.where(low, swap(three), 0.0)], axis=1
            ).astype(BF16)

    def fold(wide):
        both = wide[:, :128] + wide[:, 128:]
        return both + swap(both)

    finish(wait_x)
    fill(block0)

    finish(wait_r + wait_c)
    degree_i = row_parts[0]
    for q in range(1, inner):
        degree_i = degree_i + row_parts[q]
    degree_j = col_parts[0]
    for d in range(1, lines):
        degree_j = degree_j + col_parts[d]
    root_j = jnp.sqrt(degree_j)
    inv_j = 1.0 / root_j
    volume_part = jnp.sum(degree_j)
    own = jnp.zeros((1, rows), F32)
    for q in range(inner):
        own = own + jnp.where(mine_b == q, degree_i[q : q + 1], 0.0)
        column = jnp.broadcast_to(degree_i[q : q + 1], (128, rows)).T
        inv_i = jnp.concatenate([1.0 / jnp.sqrt(column)] * (width // 128), axis=1)
        span = slice(q * rows, (q + 1) * rows)
        one, two, three = split3(kern[span, :] * inv_i * inv_j)
        terms[0, span, :] = one
        terms[1, span, :] = two
        terms[2, span, :] = three
    own_root = pack_rows(jnp.sqrt(jnp.broadcast_to(own, (128, rows)).T))
    root_terms = jnp.concatenate(
        [t.astype(F32) for t in split3(root_j)] + [jnp.zeros((13, width), F32)], axis=0
    ).astype(BF16)
    first_row = lax.broadcasted_iota(jnp.int32, (8, 128), 0) == 0

    def apply(send, part):
        block = stacked[...]
        proj = jnp.sum(fold(dot(root_terms, block, (1, 0))), axis=0, keepdims=True)
        tail = jnp.where(first_row, jnp.broadcast_to(proj, (8, 128)), volume_part)
        waits = []
        for step in list(range(1, inner)) + [0]:
            slot, target = inner_peer(step)
            span = pl.ds(pl.multiple_of(slot * rows, 32), rows)
            wide = (
                dot(terms[2, span, :], block, (1, 0))
                + dot(terms[1, span, :], block, (1, 0))
                + dot(terms[0, span, :], block, (1, 0))
            )
            place = part.at[mine_b] if step == 0 else send.at[step]
            place[:half, :] = pack_rows(fold(wide))
            place[half:, :] = tail
            if step:
                index = count[0]
                count[0] += 1
                copy = pltpu.make_async_remote_copy(
                    src_ref=send.at[step], dst_ref=part.at[mine_b],
                    send_sem=send_sem.at[index], recv_sem=recv_sem.at[index],
                    device_id={"row": target}, device_id_type=MESH,
                )
                copy.start()
                started.append(copy)
                source = inner_peer(inner - step)[0]
                waits.append(
                    pltpu.make_async_remote_copy(
                        src_ref=send.at[step], dst_ref=part.at[source],
                        send_sem=send_sem.at[index], recv_sem=recv_sem.at[index],
                        device_id={"row": target}, device_id_type=MESH,
                    )
                )
        return waits

    def collect(part):
        total = part[0]
        for q in range(1, inner):
            total = total + part[q]
        proj = total[half : half + 1]
        volume = total[half + 1 : half + 2]
        return total[:half] - own_root * (proj / volume)

    finish(apply(send1, part1))
    block1[mine_a] = collect(part1)
    finish(exchange(lines, line_peer, mine_a, block1))

    gram = local_gram(block1[0])
    for d in range(1, lines):
        gram = gram + local_gram(block1[d])
    gram1[mine_b] = gram
    wait_g = exchange(inner, inner_peer, mine_b, gram1)
    fill(block1)
    wait_y = apply(send2, part2)
    finish(wait_g)
    gram = gram1[0]
    for q in range(1, inner):
        gram = gram + gram1[q]
    factor = inverse_factor(gram)
    finish(wait_y)
    image = dot(collect(part2), factor, (1, 1), HIGHEST)

    gram2[mine_b] = local_gram(image)
    finish(exchange(inner, inner_peer, mine_b, gram2))
    gram = gram2[0]
    for q in range(1, inner):
        gram = gram + gram2[q]
    gram3[mine_a] = gram
    finish(exchange(lines, line_peer, mine_a, gram3))
    gram = gram3[0]
    for d in range(1, lines):
        gram = gram + gram3[d]
    basis = dot(image, inverse_factor(gram), (1, 1), HIGHEST)
    basis = basis * math.sqrt(rows * lines * inner)
    out_ref[:half, :] = basis[:, :64]
    out_ref[half:, :] = basis[:, 64:]
    for copy in started:
        copy.wait_send()


def shards(prints_a, prints_b, prints_c, prints_d, start_block):
    rows, columns = start_block.shape
    devices = lax.axis_size("row")
    inner = 1
    while inner * inner < devices or devices % inner:
        inner += 1
    lines = devices // inner
    words = jnp.concatenate(
        [prints_a.T, prints_b.T, prints_c.T, prints_d.T], axis=0
    )
    depth = words.shape[0]
    copies = 6 * (inner - 1) + 5 * (lines - 1)
    half = rows // 2
    return pl.pallas_call(
        functools.partial(kernel, lines, inner, rows),
        out_shape=jax.ShapeDtypeStruct((rows, columns), F32),
        in_specs=[pl.BlockSpec(memory_space=pltpu.VMEM)] * 2,
        out_specs=pl.BlockSpec(memory_space=pltpu.VMEM),
        scratch_shapes=[
            pltpu.VMEM((inner, depth, rows), jnp.int32),
            pltpu.VMEM((lines, depth, rows), jnp.int32),
            pltpu.VMEM((lines, half, 128), F32),
            pltpu.VMEM((lines, half, 128), F32),
            pltpu.VMEM((inner * rows, lines * rows), F32),
            pltpu.VMEM((3, inner * rows, lines * rows), BF16),
            pltpu.VMEM((lines * rows, 256), BF16),
            pltpu.VMEM((inner, inner, rows), F32),
            pltpu.VMEM((lines, 1, lines * rows), F32),
            pltpu.VMEM((inner, half + 8, 128), F32),
            pltpu.VMEM((inner, half + 8, 128), F32),
            pltpu.VMEM((inner, half + 8, 128), F32),
            pltpu.VMEM((inner, half + 8, 128), F32),
            pltpu.VMEM((inner, 32, 128), F32),
            pltpu.VMEM((inner, 32, 128), F32),
            pltpu.VMEM((lines, 32, 128), F32),
            pltpu.SemaphoreType.DMA((copies,)),
            pltpu.SemaphoreType.DMA((copies,)),
        ],
        compiler_params=pltpu.CompilerParams(
            collective_id=0, has_side_effects=True, vmem_limit_bytes=56 * 2**20
        ),
    )(words, start_block)


def solution(mesh):
    placed = (P(("grp", "row"), None),) * 5
    return jax.shard_map(
        shards, mesh=mesh, in_specs=placed, out_specs=P(("grp", "row"), None), check_vma=False
    )
```

profile of v0, /device:TPU:0, one launch (start us, length us, event | category | flops | bytes accessed | tf_op | source)
XLA Modules:
  0.0 54.7 jit_solution(14962958133539803089)
XLA Ops:
  0.0 0.0 copy-start
  0.0 0.7 %copy-done = s32[160,4]{0,1:T(4,128)S(1)} copy-done((s32[160,4]{0,1:T(4,128)S(1)}, s32[160,4]{0,1:T(4,128)}, u32[]{:S(2)}) %copy-start) | copy-done | bytes 2584
  0.7 1.3 %pad_add_fusion.words_ref = s32[16,160]{1,0:T(8,128)} fusion(s32[4,160]{1,0:T(4,128)S(1)} %bitcast.4, s32[4,160]{1,0:T(4,128)} %bitcast.5, s32[4,160]{1,0:T(4,128)} %bitcast.6, s32[4,160]{1,0:T(4,128)} %bitcast.7), kind=kLoop, calls=%fused_computation | loop fusion | flops 7680 | bytes 20480 | tf_op jit(solution)/shard_map/concatenate | solution.py:311
  2.0 1.6 %copy.6.start_ref = f32[160,64]{1,0:T(8,128)} copy(f32[160,64]{0,1:T(8,128)} %param.9) | data formatting | bytes 81920 | tf_op args[4]
  3.6 49.6 %shard_map.55 = f32[160,64]{1,0:T(8,128)} custom-call(s32[16,160]{1,0:T(8,128)} %pad_add_fusion.words_ref, f32[160,64]{1,0:T(8,128)} %copy.6.start_ref), custom_call_target="tpu_custom_call" | custom-call | tf_op jit(solution)/shard_map/pallas_call | solution.py:317
  53.1 1.6 %copy.7 = f32[160,64]{0,1:T(8,128)} copy(f32[160,64]{1,0:T(8,128)} %shard_map.55) | data formatting | bytes 81920 | tf_op jit(solution)/shard_map/pallas_call | solution.py:317
Async XLA Ops:
  0.0 0.7 %copy-start = (s32[160,4]{0,1:T(4,128)S(1)}, s32[160,4]{0,1:T(4,128)}, u32[]{:S(2)}) copy-start(s32[160,4]{0,1:T(4,128)} %param.8) | copy-start | bytes 7684
where the time goes:
time: 55 us; the launch traced here: 54.7 us
  Pallas kernels  49.6 us (90%)
  local copies, waits for them, and re-layouts  3.84 us (7%)
  other arithmetic  1.33 us (2%)
    pallas_call x1, Pallas kernels, shards(): pl.pallas_call(functools.partial(kernel, lines, inner, rows), out_shape=j...  49.6 us
    unnamed x3, local copies, waits for them, and re-layouts  2.24 us
    pallas_call x1, local copies, waits for them, and re-layouts, shards(): pl.pallas_call(functools.partial(kernel, lines, inner, rows), out_shape=j...  1.6 us
    concatenate x1, other arithmetic, shards(): jnp.concatenate([prints_a.T, prints_b.T, prints_c.T, prints_d.T], axis=0)  1.33 us

commit v1 on v0

--- a/solution.py
+++ b/solution.py
@@ -56,34 +56,42 @@
 
 
 def inverse_factor(gram):
-    size = 64
+    size, panels = 64, 8
     rows = lax.broadcasted_iota(jnp.int32, (size, 128), 0)
     lanes = lax.broadcasted_iota(jnp.int32, (size, 128), 1)
     low = lanes < size
+    index = lax.broadcasted_iota(jnp.int32, (8, 128), 0)
     square = jnp.concatenate([gram, swap(gram)], axis=0)
     work = jnp.where(low, square, (lanes - size == rows).astype(F32))
-    done = []
-    for j in range(size):
-        start = (j // 8) * 8
-        top = j - start
-        row = work[top : top + 1, :]
-        column = jnp.broadcast_to(work[:, j : j + 1], work.shape)
-        pivot = 1.0 / column[top : top + 1, :]
-        index = lax.broadcasted_iota(jnp.int32, work.shape, 0) + start
-        work = work - jnp.where(index > j, column, 0.0) * (pivot * row)
-        if top == 7:
-            done.append(work[:8])
-            work = work[8:]
-    work = jnp.concatenate(done, axis=0)
-    diag = jnp.sum(jnp.where(lanes == rows, work, 0.0), axis=1, keepdims=True)
-    inverse = work * (1.0 / jnp.sqrt(diag))
+    tiles = [work[8 * i : 8 * i + 8] for i in range(panels)]
+    for p in range(panels):
+        spread = [
+            [jnp.broadcast_to(tile[:, k : k + 1], (8, 128)) for k in range(8 * p, 8 * p + 8)]
+            for tile in tiles[p:]
+        ]
+        pivots = jnp.zeros((8, 128), F32)
+        for j in range(8):
+            head = [jnp.broadcast_to(column[j : j + 1], (8, 128)) for column in spread[0]]
+            pivot = 1.0 / head[j]
+            pivots = jnp.where(index == j, pivot, pivots)
+            line = jnp.broadcast_to(tiles[p][j : j + 1], (8, 128))
+            for i in range(p, panels):
+                columns = spread[i - p]
+                ratio = columns[j] * pivot
+                if i == p:
+                    ratio = jnp.where(index > j, ratio, 0.0)
+                for k in range(j + 1, 8):
+                    columns[k] = columns[k] - ratio * head[k]
+                tiles[i] = tiles[i] - ratio * line
+        tiles[p] = tiles[p] * jnp.sqrt(pivots)
+    inverse = jnp.concatenate(tiles, axis=0)
     return jnp.concatenate(
         [jnp.where(low, swap(inverse), 0.0), jnp.where(low, 0.0, inverse)], axis=0
     )
 
 
 def kernel(
-    lines, inner, rows, words_ref, start_ref, out_ref,
+    lines, inner, rows, a_ref, b_ref, c_ref, d_ref, start_ref, out_ref,
     words_i, words_j, block0, block1, kern, terms, stacked,
     row_parts, col_parts, send1, send2, part1, part2, gram1, gram2, gram3,
     send_sem, recv_sem,
@@ -138,10 +146,12 @@
         for copy in waits:
             copy.wait_recv()
 
-    words_i[mine_b] = words_ref[...]
-    words_j[mine_a] = words_ref[...]
-    start = start_ref[...]
-    block0[mine_a] = jnp.concatenate([start[:half], start[half:]], axis=1)
+    taken = 0
+    for ref in (a_ref, b_ref, c_ref, d_ref):
+        words_i[mine_b, taken : taken + ref.shape[0], :] = ref[...]
+        words_j[mine_a, taken : taken + ref.shape[0], :] = ref[...]
+        taken += ref.shape[0]
+    block0[mine_a] = pack_rows(jnp.concatenate([start_ref[...]] * 2, axis=0).T)
 
     pl.semaphore_wait(barrier, inner + lines - 2)
     wait_j = exchange(lines, line_peer, mine_a, words_j)
@@ -176,23 +186,23 @@
 
     low = low_lanes((half, 128))
 
-    def fill(block):
-        for d in range(lines):
-            one, two, three = [t.astype(F32) for t in split3(block[d])]
-            base = d * rows
-            stacked[base : base + half, :] = jnp.concatenate(
-                [jnp.where(low, one, swap(two)), jnp.where(low, three, 0.0)], axis=1
-            ).astype(BF16)
-            stacked[base + half : base + rows, :] = jnp.concatenate(
-                [jnp.where(low, swap(one), two), jnp.where(low, swap(three), 0.0)], axis=1
-            ).astype(BF16)
+    def fill(block, slot):
+        one, two, three = [t.astype(F32) for t in split3(block[slot])]
+        base = slot * rows
+        stacked[pl.ds(pl.multiple_of(base, 16), half), :] = jnp.concatenate(
+            [jnp.where(low, one, swap(two)), jnp.where(low, three, 0.0)], axis=1
+        ).astype(BF16)
+        stacked[pl.ds(pl.multiple_of(base + half, 16), half), :] = jnp.concatenate(
+            [jnp.where(low, swap(one), two), jnp.where(low, swap(three), 0.0)], axis=1
+        ).astype(BF16)
 
     def fold(wide):
         both = wide[:, :128] + wide[:, 128:]
         return both + swap(both)
 
     finish(wait_x)
-    fill(block0)
+    for d in range(lines):
+        fill(block0, d)
 
     finish(wait_r + wait_c)
     degree_i = row_parts[0]
@@ -266,14 +276,17 @@
 
     finish(apply(send1, part1))
     block1[mine_a] = collect(part1)
-    finish(exchange(lines, line_peer, mine_a, block1))
-
-    gram = local_gram(block1[0])
-    for d in range(1, lines):
-        gram = gram + local_gram(block1[d])
+    wait_x = exchange(lines, line_peer, mine_a, block1)
+
+    gram = local_gram(block1[mine_a])
+    fill(block1, mine_a)
+    for step in range(1, lines):
+        finish(wait_x[step - 1 : step])
+        slot = line_peer(lines - step)[0]
+        gram = gram + local_gram(block1[slot])
+        fill(block1, slot)
     gram1[mine_b] = gram
     wait_g = exchange(inner, inner_peer, mine_b, gram1)
-    fill(block1)
     wait_y = apply(send2, part2)
     finish(wait_g)
     gram = gram1[0]
@@ -295,8 +308,7 @@
         gram = gram + gram3[d]
     basis = dot(image, inverse_factor(gram), (1, 1), HIGHEST)
     basis = basis * math.sqrt(rows * lines * inner)
-    out_ref[:half, :] = basis[:, :64]
-    out_ref[half:, :] = basis[:, 64:]
+    out_ref[...] = jnp.concatenate([basis, swap(basis)], axis=0).T[: out_ref.shape[0]]
     for copy in started:
         copy.wait_send()
 
@@ -308,16 +320,14 @@
     while inner * inner < devices or devices % inner:
         inner += 1
     lines = devices // inner
-    words = jnp.concatenate(
-        [prints_a.T, prints_b.T, prints_c.T, prints_d.T], axis=0
-    )
-    depth = words.shape[0]
+    words = [part.T for part in (prints_a, prints_b, prints_c, prints_d)]
+    depth = sum(part.shape[0] for part in words)
     copies = 6 * (inner - 1) + 5 * (lines - 1)
     half = rows // 2
     return pl.pallas_call(
         functools.partial(kernel, lines, inner, rows),
-        out_shape=jax.ShapeDtypeStruct((rows, columns), F32),
-        in_specs=[pl.BlockSpec(memory_space=pltpu.VMEM)] * 2,
+        out_shape=jax.ShapeDtypeStruct((columns, rows), F32),
+        in_specs=[pl.BlockSpec(memory_space=pltpu.VMEM)] * 5,
         out_specs=pl.BlockSpec(memory_space=pltpu.VMEM),
         scratch_shapes=[
             pltpu.VMEM((inner, depth, rows), jnp.int32),
@@ -342,7 +352,7 @@
         compiler_params=pltpu.CompilerParams(
             collective_id=0, has_side_effects=True, vmem_limit_bytes=56 * 2**20
         ),
-    )(words, start_block)
+    )(*words, start_block.T).T
 
 
 def solution(mesh):

time: 55 us -> 44 us (0.80)
  Pallas kernels: 49.6 us -> 42.3 us
  local copies, waits for them, and re-layouts: 3.84 us -> 1.47 us
  other arithmetic: 1.33 us -> 0 us
    pallas_call x1, Pallas kernels: 49.6 us -> 42.3 us  [shards(): pl.pallas_call(functools.partial(kernel, lines, inner, rows), out_shape=j...]
    pallas_call x1 -> x0, local copies, waits for them, and re-layouts: 1.6 us -> none  [shards(): pl.pallas_call(functools.partial(kernel, lines, inner, rows), out_shape=j...]
    concatenate x1 -> x0, other arithmetic: 1.33 us -> none  [shards(): jnp.concatenate([prints_a.T, prints_b.T, prints_c.T, prints_d.T], axis=0)]
    unnamed x3 -> x1, local copies, waits for them, and re-layouts: 2.24 us -> 1.47 us
where the time goes in v1:
time: 44 us; the launch traced here: 43.8 us
  Pallas kernels  42.3 us (96%)
  local copies, waits for them, and re-layouts  1.47 us (3%)
    pallas_call x1, Pallas kernels, shards(): pl.pallas_call(functools.partial(kernel, lines, inner, rows), out_shape=j...  42.3 us
    unnamed x1, local copies, waits for them, and re-layouts  1.47 us

profile of v1, /device:TPU:0, one launch (start us, length us, event | category | flops | bytes accessed | tf_op | source)
XLA Modules:
  0.0 43.8 jit_solution(17919300756374215458)
XLA Ops:
  0.0 42.3 %shard_map.55 = f32[64,160]{1,0:T(8,128)} custom-call(s32[4,160]{1,0:T(4,128)} %bitcast.8, s32[4,160]{1,0:T(4,128)} %bitcast.9, s32[4,160]{1,0:T(4,128)} %bitcast.10, s32[4,160]{1,0:T(4,128)} %bitcast.11, f32[64,160]{1,0:T(8,128)} %bitcast.7), custom_call_target="tpu_custom_call" | custom-call | tf_op jit(solution)/shard_map/pallas_call | solution.py:327
  42.3 1.5 %copy.7 = f32[160,64]{0,1:T(8,128)} copy(f32[160,64]{0,1:T(8,128)} %bitcast.6) | data formatting | bytes 81920

commit v2 on v1

--- a/solution.py
+++ b/solution.py
@@ -91,10 +91,10 @@
 
 
 def kernel(
-    lines, inner, rows, a_ref, b_ref, c_ref, d_ref, start_ref, out_ref,
+    lines, inner, rows, a_hbm, b_hbm, c_hbm, d_hbm, start_hbm, image_ref, gram_ref,
     words_i, words_j, block0, block1, kern, terms, stacked,
     row_parts, col_parts, send1, send2, part1, part2, gram1, gram2, gram3,
-    send_sem, recv_sem,
+    send_sem, recv_sem, load_sem, a_ref, b_ref, c_ref, d_ref, start_ref,
 ):
     me = lax.axis_index("row")
     mine_a = me // inner
@@ -115,6 +115,15 @@
         pl.semaphore_signal(barrier, 1, device_id={"row": inner_peer(step)[1]}, device_id_type=MESH)
     for step in range(1, lines):
         pl.semaphore_signal(barrier, 1, device_id={"row": line_peer(step)[1]}, device_id_type=MESH)
+
+    loads = [
+        pltpu.make_async_copy(source, target, load_sem.at[place])
+        for place, (source, target) in enumerate([
+            (a_hbm, a_ref), (b_hbm, b_ref), (c_hbm, c_ref), (d_hbm, d_ref), (start_hbm, start_ref)
+        ])
+    ]
+    for load in loads:
+        load.start()
 
     count = [0]
     started = []
@@ -146,6 +155,8 @@
         for copy in waits:
             copy.wait_recv()
 
+    for load in loads:
+        load.wait()
     taken = 0
     for ref in (a_ref, b_ref, c_ref, d_ref):
         words_i[mine_b, taken : taken + ref.shape[0], :] = ref[...]
@@ -306,11 +317,16 @@
     gram = gram3[0]
     for d in range(1, lines):
         gram = gram + gram3[d]
-    basis = dot(image, inverse_factor(gram), (1, 1), HIGHEST)
-    basis = basis * math.sqrt(rows * lines * inner)
-    out_ref[...] = jnp.concatenate([basis, swap(basis)], axis=0).T[: out_ref.shape[0]]
+    image_ref[...] = image
+    gram_ref[...] = gram
     for copy in started:
         copy.wait_send()
+
+
+def last_kernel(molecules, image_ref, gram_ref, out_ref):
+    basis = dot(image_ref[...], inverse_factor(gram_ref[...]), (1, 1), HIGHEST)
+    basis = basis * math.sqrt(molecules)
+    out_ref[...] = jnp.concatenate([basis, swap(basis)], axis=0).T[: out_ref.shape[0]]
 
 
 def shards(prints_a, prints_b, prints_c, prints_d, start_block):
@@ -324,11 +340,13 @@
     depth = sum(part.shape[0] for part in words)
     copies = 6 * (inner - 1) + 5 * (lines - 1)
     half = rows // 2
-    return pl.pallas_call(
+    image, gram = pl.pallas_call(
         functools.partial(kernel, lines, inner, rows),
-        out_shape=jax.ShapeDtypeStruct((columns, rows), F32),
-        in_specs=[pl.BlockSpec(memory_space=pltpu.VMEM)] * 5,
-        out_specs=pl.BlockSpec(memory_space=pltpu.VMEM),
+        out_shape=(
+            jax.ShapeDtypeStruct((half, 128), F32), jax.ShapeDtypeStruct((32, 128), F32)
+        ),
+        in_specs=[pl.BlockSpec(memory_space=pl.ANY)] * 5,
+        out_specs=(pl.BlockSpec(memory_space=pltpu.VMEM),) * 2,
         scratch_shapes=[
             pltpu.VMEM((inner, depth, rows), jnp.int32),
             pltpu.VMEM((lines, depth, rows), jnp.int32),
@@ -348,11 +366,20 @@
             pltpu.VMEM((lines, 32, 128), F32),
             pltpu.SemaphoreType.DMA((copies,)),
             pltpu.SemaphoreType.DMA((copies,)),
-        ],
+            pltpu.SemaphoreType.DMA((5,)),
+        ]
+        + [pltpu.VMEM(part.shape, jnp.int32) for part in words]
+        + [pltpu.VMEM((columns, rows), F32)],
         compiler_params=pltpu.CompilerParams(
             collective_id=0, has_side_effects=True, vmem_limit_bytes=56 * 2**20
         ),
-    )(*words, start_block.T).T
+    )(*words, start_block.T)
+    return pl.pallas_call(
+        functools.partial(last_kernel, rows * devices),
+        out_shape=jax.ShapeDtypeStruct((columns, rows), F32),
+        in_specs=[pl.BlockSpec(memory_space=pltpu.VMEM)] * 2,
+        out_specs=pl.BlockSpec(memory_space=pltpu.VMEM),
+    )(image, gram).T
 
 
 def solution(mesh):

time: 44 us -> 43 us (0.977)
  local copies, waits for them, and re-layouts: 1.47 us -> 0 us
  Pallas kernels: 42.3 us -> 42.8 us
    unnamed x1 -> x0, local copies, waits for them, and re-layouts: 1.47 us -> none
    pallas_call x1 -> x2, Pallas kernels: 42.3 us -> 42.8 us  [the longest x1 39.2 us: shards(): pl.pallas_call(functools.partial(kernel, lines, inner, rows), out_shape=(...]
where the time goes in v2:
time: 43 us; the launch traced here: 42.8 us
  Pallas kernels  42.8 us (100%)
    pallas_call x1, Pallas kernels, shards(): pl.pallas_call(functools.partial(kernel, lines, inner, rows), out_shape=(...  39.2 us
    pallas_call x1, Pallas kernels, shards(): pl.pallas_call(functools.partial(last_kernel, rows * devices), out_shape=...  3.62 us

profile of v2, /device:TPU:0, one launch (start us, length us, event | category | flops | bytes accessed | tf_op | source)
XLA Modules:
  0.0 42.8 jit_solution(4391509333265906603)
XLA Ops:
  0.0 39.2 %shard_map.55 = (f32[80,128]{1,0:T(8,128)}, f32[32,128]{1,0:T(8,128)}) custom-call(s32[4,160]{1,0:T(4,128)} %bitcast.7, s32[4,160]{1,0:T(4,128)} %bitcast.8, s32[4,160]{1,0:T(4,128)} %bitcast.9, s32[4,160]{1,0:T(4,128)} %bitcast.10, f32[64,160]{1,0:T(8,128)} %bitcast.6), custom_call_target="tpu_custom_call" | custom-call | tf_op jit(solution)/shard_map/pallas_call | solution.py:343
  39.2 3.6 %shard_map.56 = f32[64,160]{1,0:T(8,128)} custom-call(f32[80,128]{1,0:T(8,128)} %get-tuple-element.7.image_ref, f32[32,128]{1,0:T(8,128)} %get-tuple-element.8.gram_ref), custom_call_target="tpu_custom_call" | custom-call | tf_op jit(solution)/shard_map/pallas_call | solution.py:377
